TPU v7x, 512 devices: a whole 4x4x16 slice. The times are simulated.
512 devices in a mesh: blk: 128 (over z, x, y_hi), head: 4 (over y_lo, core).
Axes of the slice: x: 4, y: 4 (y_hi: 2, y_lo: 2; y = y_hi * 2 + y_lo), z: 16, core: 2. Of those that a mesh axis runs over, the one named last changes fastest.
Arguments:
- vertices: bfloat16 [16384, 1024], P('blk'), may hold values from -6 to 6
- grad_out: bfloat16 [16384, 1024], P('blk'), may hold values from -6 to 6
- w_query: bfloat16 [1024, 1024], P(None, 'head'), may hold values from -0.1875 to 0.1875
- w_key: bfloat16 [1024, 1024], P(None, 'head'), may hold values from -0.1875 to 0.1875
- w_value: bfloat16 [1024, 1024], P(None, 'head'), may hold values from -0.1875 to 0.1875
- w_out: bfloat16 [1024, 1024], P('head'), may hold values from -0.1875 to 0.1875
- pair_bins: int32 [512, 20], P('blk'), may hold values from 0 to 31
- bias_table: float32 [4, 32], replicated, may hold values from -4 to 310
- head_index: int32 [16], P('head'), may hold values from 0 to 3
Outputs:
- grad_vertices: bfloat16 [16384, 1024], P('blk', 'head')
All inputs are finite; a program needn't handle non-finite values.
Results may differ from a plain program's by a relative error of at most 0.017.
Values may be sent and summed in bfloat16 or wider, within the bound.
A program may use at most 64 MiB of HBM per device.

v0:
```python
import jax
import jax.numpy as jnp
from jax import lax
from jax.sharding import PartitionSpec as P

HEAD_DIM = 64
REACH = 2
GROUP = 32


def from_behind(x, axis, by):
    peers = lax.axis_size(axis)
    return lax.ppermute(x, axis, [(i, (i + by) % peers) for i in range(peers)])


def spread_bias(group_bias):
    count, rows_g, cols_g = group_bias.shape
    wide = jnp.broadcast_to(group_bias[:, :, None, :, None], (count, rows_g, GROUP, cols_g, GROUP))
    return wide.reshape(count, rows_g * GROUP, cols_g * GROUP)


def body(vertices, grad_out, w_query, w_key, w_value, w_out, pair_bins, bias_table, head_index):
    row_count = vertices.shape[0]
    feature_count = w_query.shape[1]
    head_count = feature_count // HEAD_DIM
    score_scale = HEAD_DIM ** (-0.5)
    per_block = row_count // GROUP
    queries = jnp.dot(vertices, w_query, preferred_element_type=jnp.float32).astype(jnp.bfloat16)
    keys_own = jnp.dot(vertices, w_key, preferred_element_type=jnp.float32).astype(jnp.bfloat16)
    values_own = jnp.dot(vertices, w_value, preferred_element_type=jnp.float32).astype(jnp.bfloat16)
    grad_attn = jnp.einsum("ie,fe->if", grad_out, w_out, preferred_element_type=jnp.float32).astype(
        jnp.bfloat16
    )
    picker = (
        head_index[:, None] == jnp.arange(bias_table.shape[0], dtype=jnp.int32)[None, :]
    ).astype(jnp.float32)
    head_table = jnp.dot(picker, bias_table, precision=lax.Precision.HIGHEST)
    levels = (
        pair_bins[:, :, None] == jnp.arange(bias_table.shape[1], dtype=jnp.int32)[None, None, :]
    ).astype(jnp.float32)
    group_bias = jnp.einsum("gcb,hb->hgc", levels, head_table, precision=lax.Precision.HIGHEST)
    query3 = queries.reshape(row_count, head_count, HEAD_DIM)
    grad3 = grad_attn.reshape(row_count, head_count, HEAD_DIM)
    offset_list = list(range(-REACH, REACH + 1))
    own_pair = jnp.stack([keys_own, values_own])
    window = {0: own_pair}
    moving = own_pair
    for distance in range(1, REACH + 1):
        moving = from_behind(moving, "blk", 1)
        window[-distance] = moving
    moving = own_pair
    for distance in range(1, REACH + 1):
        moving = from_behind(moving, "blk", -1)
        window[distance] = moving
    held = {}
    row_peak = None
    row_total = None
    for offset in offset_list:
        first = (offset + REACH) * per_block
        bias = spread_bias(group_bias[:, :, first : first + per_block])
        tile_key3 = window[offset][0].reshape(row_count, head_count, HEAD_DIM)
        scores = (
            jnp.einsum("qhd,khd->hqk", query3, tile_key3, preferred_element_type=jnp.float32)
            * score_scale
            + bias
        )
        held[offset] = scores
        tile_peak = jnp.max(scores, axis=2, keepdims=True)
        if row_peak is None:
            row_peak = tile_peak
            row_total = jnp.sum(jnp.exp(scores - row_peak), axis=2, keepdims=True)
        else:
            new_peak = jnp.maximum(row_peak, tile_peak)
            row_total = row_total * jnp.exp(row_peak - new_peak) + jnp.sum(
                jnp.exp(scores - new_peak), axis=2, keepdims=True
            )
            row_peak = new_peak

    def scores_again(offset):
        return held[offset]

    output_sum = jnp.zeros((row_count, head_count, HEAD_DIM), jnp.float32)
    for offset in offset_list:
        attend_low = (jnp.exp(scores_again(offset) - row_peak) / row_total).astype(jnp.bfloat16)
        value3 = window[offset][1].reshape(row_count, head_count, HEAD_DIM)
        output_sum = output_sum + jnp.einsum(
            "hqk,khd->qhd", attend_low, value3, preferred_element_type=jnp.float32
        )
    output = output_sum.astype(jnp.bfloat16)
    row_dot = jnp.sum(grad3.astype(jnp.float32) * output.astype(jnp.float32), axis=2)
    query_grad = jnp.zeros((row_count, head_count, HEAD_DIM), jnp.float32)
    tile_parts = {}
    for offset in offset_list:
        pair = window[offset]
        key3 = pair[0].reshape(row_count, head_count, HEAD_DIM)
        value3 = pair[1].reshape(row_count, head_count, HEAD_DIM)
        attend = jnp.exp(scores_again(offset) - row_peak) / row_total
        attend_low = attend.astype(jnp.bfloat16)
        grad_weights = jnp.einsum("qhd,khd->hqk", grad3, value3, preferred_element_type=jnp.float32)
        grad_scores = (attend * (grad_weights - row_dot.T[:, :, None])).astype(jnp.bfloat16)
        query_grad = query_grad + jnp.einsum(
            "hqk,khd->qhd", grad_scores, key3, preferred_element_type=jnp.float32
        )
        key_term = (
            jnp.einsum("hqk,qhd->khd", grad_scores, query3, preferred_element_type=jnp.float32)
            * score_scale
        )
        value_term = jnp.einsum(
            "hqk,qhd->khd", attend_low, grad3, preferred_element_type=jnp.float32
        )
        tile_parts[offset] = jnp.stack(
            [
                key_term.reshape(row_count, feature_count),
                value_term.reshape(row_count, feature_count),
            ]
        )
    gathered = tile_parts[0]
    moving = tile_parts[-1]
    distance = 2
    moving = (
        from_behind(moving.astype(jnp.bfloat16), "blk", 1).astype(moving.dtype)
        + tile_parts[-distance]
    )
    gathered = gathered + from_behind(moving, "blk", -REACH)
    moving = tile_parts[1]
    distance = 2
    moving = (
        from_behind(moving.astype(jnp.bfloat16), "blk", -1).astype(moving.dtype)
        + tile_parts[distance]
    )
    gathered = gathered + from_behind(moving, "blk", REACH)
    grad_query = (query_grad * score_scale).astype(jnp.bfloat16).reshape(row_count, feature_count)
    grad_key = gathered[0].astype(jnp.bfloat16)
    grad_value = gathered[1].astype(jnp.bfloat16)
    partial_sum = jnp.einsum("if,ef->ie", grad_query, w_query, preferred_element_type=jnp.float32)
    partial_sum = partial_sum + jnp.einsum(
        "if,ef->ie", grad_key, w_key, preferred_element_type=jnp.float32
    )
    partial_sum = partial_sum + jnp.einsum(
        "if,ef->ie", grad_value, w_value, preferred_element_type=jnp.float32
    )
    return lax.psum_scatter(partial_sum, "head", scatter_dimension=1, tiled=True).astype(
        jnp.bfloat16
    )


def solution(mesh):
    in_specs = (
        P("blk", None),
        P("blk", None),
        P(None, "head"),
        P(None, "head"),
        P(None, "head"),
        P("head", None),
        P("blk", None),
        P(),
        P("head"),
    )
    out_specs = P("blk", "head")
    return jax.shard_map(body, mesh=mesh, in_specs=in_specs, out_specs=out_specs, check_vma=False)
```

profile of v0, /device:TPU:1, one launch (start us, length us, event | category | flops | bytes accessed | tf_op | source)
XLA Modules:
  0.0 123.2 jit_solution(2806226862164625748)
XLA Ops:
  6.5 1.5 %convolution_convert_fusion.3 = bf16[128,256]{1,0:T(8,128)(2,1)S(1)} fusion(bf16[128,1024]{1,0:T(8,128)(2,1)} %param.9, bf16[1024,256]{1,0:T(8,128)(2,1)} %param.12), kind=kOutput, calls=%fused_computation.45 | convolution fusion | flops 67141632 | bytes 851968 | tf_op jit(solution)/shard_map/dot_general | solution.py:29
  8.9 5.6 %collective-permute-start = (bf16[2,128,256]{2,1,0:T(8,128)(2,1)}, bf16[2,128,256]{2,1,0:T(8,128)(2,1)}, u32[]{:S(2)}, u32[]{:S(2)}) collective-permute-start(bf16[2,128,256]{2,1,0:T(8,128)(2,1)} %pad_maximum_fusion), channel_id=1, source_target_pairs={{0,4},{4,8},{8,12},{12,16},{16,20},{20,24},{24,28},{28,32},{32,36}... | collective-permute-start | bytes 393224 | tf_op jit(solution)/shard_map/ppermute | solution.py:13
  14.6 13.0 %collective-permute-start.2 = (bf16[2,128,256]{2,1,0:T(8,128)(2,1)}, bf16[2,128,256]{2,1,0:T(8,128)(2,1)}, u32[]{:S(2)}, u32[]{:S(2)}) collective-permute-start(bf16[2,128,256]{2,1,0:T(8,128)(2,1)} %pad_maximum_fusion), channel_id=1, source_target_pairs={{0,508},{4,0},{8,4},{12,8},{16,12},{20,16},{24,20},{28,24},{32,28}... | collective-permute-start | bytes 393224 | tf_op jit(solution)/shard_map/ppermute | solution.py:13
  27.8 0.7 copy.97
  34.5 1.4 %convolution_convert_fusion = bf16[128,256]{1,0:T(8,128)(2,1)S(1)} fusion(bf16[128,1024]{1,0:T(8,128)(2,1)} %param.10, bf16[256,1024]{1,0:T(8,128)(2,1)} %param.14), kind=kOutput, calls=%fused_computation.42 | convolution fusion | flops 67141632 | bytes 851968 | tf_op jit(solution)/shard_map/ie,fe->if/dot_general | solution.py:31
  36.3 0.9 fusion.42
  37.3 0.9 fusion.44
  38.3 0.7 copy.95
  39.1 0.7 copy.99
  40.0 1.9 %collective-permute-start.1 = (bf16[2,128,256]{2,1,0:T(8,128)(2,1)}, bf16[2,128,256]{2,1,0:T(8,128)(2,1)S(1)}, u32[]{:S(2)}, u32[]{:S(2)}) collective-permute-start(bf16[2,128,256]{2,1,0:T(8,128)(2,1)} %collective-permute-done), channel_id=1, source_target_pairs={{0,4},{4,8},{8,12},{12,16},{16,20},{20,24},{24,28},{28,32},{32,36}... | collective-permute-start | bytes 393224 | tf_op jit(solution)/shard_map/ppermute | solution.py:13
  42.0 9.1 %collective-permute-start.3 = (bf16[2,128,256]{2,1,0:T(8,128)(2,1)}, bf16[2,128,256]{2,1,0:T(8,128)(2,1)S(1)}, u32[]{:S(2)}, u32[]{:S(2)}) collective-permute-start(bf16[2,128,256]{2,1,0:T(8,128)(2,1)} %collective-permute-done.2), channel_id=1, source_target_pairs={{0,508},{4,0},{8,4},{12,8},{16,12},{20,16},{24,20},{28,24},{32,28}... | collective-permute-start | bytes 393224 | tf_op jit(solution)/shard_map/ppermute | solution.py:13
  51.9 1.4 %collective-permute-done.3 = bf16[2,128,256]{2,1,0:T(8,128)(2,1)S(1)} collective-permute-done((bf16[2,128,256]{2,1,0:T(8,128)(2,1)}, bf16[2,128,256]{2,1,0:T(8,128)(2,1)S(1)}, u32[]{:S(2)}, u32[]{:S(2)}) %collective-permute-start.3) | collective-permute-done | bytes 131104 | tf_op jit(solution)/shard_map/ppermute | solution.py:13
  54.7 0.7 copy-done.11
  56.7 0.7 copy-done.12
  60.6 1.9 %collective-permute-start.4 = (bf16[2,128,256]{1,2,0:T(8,128)(2,1)S(1)}, bf16[2,128,256]{1,2,0:T(8,128)(2,1)S(1)}, u32[]{:S(2)}, u32[]{:S(2)}) collective-permute-start(bf16[2,128,256]{1,2,0:T(8,128)(2,1)S(1)} %pad_maximum_fusion.1), channel_id=1, source_target_pairs={{0,4},{4,8},{8,12},{12,16},{16,20},{20,24},{24,28},{28,32},{32,36}... | collective-permute-start | bytes 393224 | tf_op jit(solution)/shard_map/ppermute | solution.py:13
  63.0 9.5 %collective-permute-start.6 = (bf16[2,128,256]{1,2,0:T(8,128)(2,1)S(1)}, bf16[2,128,256]{1,2,0:T(8,128)(2,1)S(1)}, u32[]{:S(2)}, u32[]{:S(2)}) collective-permute-start(bf16[2,128,256]{1,2,0:T(8,128)(2,1)S(1)} %pad_maximum_fusion.2), channel_id=1, source_target_pairs={{0,508},{4,0},{8,4},{12,8},{16,12},{20,16},{24,20},{28,24},{32,28}... | collective-permute-start | bytes 393224 | tf_op jit(solution)/shard_map/ppermute | solution.py:13
  73.1 0.7 copy-done.7
  74.3 2.2 %collective-permute-start.5 = (f32[2,128,256]{1,2,0:T(8,128)S(1)}, f32[2,128,256]{1,2,0:T(8,128)S(1)}, u32[]{:S(2)}, u32[]{:S(2)}) collective-permute-start(f32[2,128,256]{1,2,0:T(8,128)S(1)} %maximum_add_fusion.1), channel_id=1, source_target_pairs={{0,504},{4,508},{8,0},{12,4},{16,8},{20,12},{24,16},{28,20},{32,24... | collective-permute-start | bytes 786440 | tf_op jit(solution)/shard_map/ppermute | solution.py:13
  76.6 3.1 %collective-permute-start.7 = (f32[2,128,256]{1,2,0:T(8,128)S(1)}, f32[2,128,256]{1,2,0:T(8,128)S(1)}, u32[]{:S(2)}, u32[]{:S(2)}) collective-permute-start(f32[2,128,256]{1,2,0:T(8,128)S(1)} %maximum_add_fusion.2), channel_id=1, source_target_pairs={{0,8},{4,12},{8,16},{12,20},{16,24},{20,28},{24,32},{28,36},{32,40... | collective-permute-start | bytes 786440 | tf_op jit(solution)/shard_map/ppermute | solution.py:13
  80.2 1.3 %collective-permute-done.5 = f32[2,128,256]{1,2,0:T(8,128)S(1)} collective-permute-done((f32[2,128,256]{1,2,0:T(8,128)S(1)}, f32[2,128,256]{1,2,0:T(8,128)S(1)}, u32[]{:S(2)}, u32[]{:S(2)}) %collective-permute-start.5) | collective-permute-done | bytes 262176 | tf_op jit(solution)/shard_map/ppermute | solution.py:13
  81.4 5.6 %collective-permute-done.7 = f32[2,128,256]{1,2,0:T(8,128)S(1)} collective-permute-done((f32[2,128,256]{1,2,0:T(8,128)S(1)}, f32[2,128,256]{1,2,0:T(8,128)S(1)}, u32[]{:S(2)}, u32[]{:S(2)}) %collective-permute-start.7) | collective-permute-done | bytes 262176 | tf_op jit(solution)/shard_map/ppermute | solution.py:13
  87.4 1.1 convolution_add_fusion
  88.5 26.3 %reduce-scatter.2.cloned.1.call-done = f32[128,256]{1,0:T(8,128)} async-done(((f32[128,1024]{1,0:T(8,128)}), f32[128,256]{1,0:T(8,128)}) %reduce-scatter.2.cloned.1.call-update) | async-done | bytes 131088 | tf_op jit(solution)/shard_map/reduce_scatter | solution.py:142
  114.8 1.5 %convert_element_type.99 = bf16[128,256]{1,0:T(8,128)(2,1)} convert(f32[128,256]{1,0:T(8,128)} %reduce-scatter.2.cloned.1.call-done) | non-fusion elementwise | flops 32768 | bytes 196608 | tf_op jit(solution)/shard_map/convert_element_type | solution.py:142
  (111 shorter events, 16.7 us)
Async XLA Ops:
  6.5 22.0 %copy-start = (bf16[1024,256]{1,0:T(8,128)(2,1)S(1)}, bf16[1024,256]{1,0:T(8,128)(2,1)}, u32[]{:S(2)}) copy-start(bf16[1024,256]{1,0:T(8,128)(2,1)} %param.11) | copy-start | bytes 1572868
  6.5 1.5 %copy-start.1 = (bf16[128,1024]{1,0:T(8,128)(2,1)S(1)}, bf16[128,1024]{1,0:T(8,128)(2,1)}, u32[]{:S(2)}) copy-start(bf16[128,1024]{1,0:T(8,128)(2,1)} %param.9) | copy-start | bytes 786436
  6.5 1.5 %copy-start.3 = (bf16[1024,256]{1,0:T(8,128)(2,1)S(1)}, bf16[1024,256]{1,0:T(8,128)(2,1)}, u32[]{:S(2)}) copy-start(bf16[1024,256]{1,0:T(8,128)(2,1)} %param.13) | copy-start | bytes 1572868
  6.5 108.3 %reduce-scatter.2.cloned.1.call-start = ((), (), s32[]{:S(2)}) async-start(), calls=%async_computation.1 | async-start | bytes 655360 | tf_op jit(solution)/shard_map/reduce_scatter | solution.py:142
  8.9 28.4 %collective-permute-start = (bf16[2,128,256]{2,1,0:T(8,128)(2,1)}, bf16[2,128,256]{2,1,0:T(8,128)(2,1)}, u32[]{:S(2)}, u32[]{:S(2)}) collective-permute-start(bf16[2,128,256]{2,1,0:T(8,128)(2,1)} %pad_maximum_fusion), channel_id=1, source_target_pairs={{0,4},{4,8},{8,12},{12,16},{16,20},{20,24},{24,28},{28,32},{32,36}... | collective-permute-start | bytes 393224 | tf_op jit(solution)/shard_map/ppermute | solution.py:13
  14.6 21.7 %collective-permute-start.2 = (bf16[2,128,256]{2,1,0:T(8,128)(2,1)}, bf16[2,128,256]{2,1,0:T(8,128)(2,1)}, u32[]{:S(2)}, u32[]{:S(2)}) collective-permute-start(bf16[2,128,256]{2,1,0:T(8,128)(2,1)} %pad_maximum_fusion), channel_id=1, source_target_pairs={{0,508},{4,0},{8,4},{12,8},{16,12},{20,16},{24,20},{28,24},{32,28}... | collective-permute-start | bytes 393224 | tf_op jit(solution)/shard_map/ppermute | solution.py:13
  27.7 8.3 %copy-start.4 = (bf16[128,256]{0,1:T(8,128)(2,1)}, bf16[128,256]{0,1:T(8,128)(2,1)S(1)}, u32[]{:S(2)}) copy-start(bf16[128,256]{0,1:T(8,128)(2,1)S(1)} %copy.86) | copy-start | bytes 196612
  28.7 0.7 copy-start.13
  29.4 0.7 copy-start.14
  37.3 2.5 %copy-start.6 = (bf16[1,128,256]{1,2,0:T(8,128)(2,1)}, bf16[1,128,256]{1,2,0:T(8,128)(2,1)S(1)}, u32[]{:S(2)}) copy-start(bf16[1,128,256]{1,2,0:T(8,128)(2,1)S(1)} %copy.88) | copy-start | bytes 196612
  38.3 12.7 %copy-start.8 = (bf16[1,128,256]{1,2,0:T(8,128)(2,1)}, bf16[1,128,256]{1,2,0:T(8,128)(2,1)S(1)}, u32[]{:S(2)}) copy-start(bf16[1,128,256]{1,2,0:T(8,128)(2,1)S(1)} %copy.84) | copy-start | bytes 196612
  40.0 11.7 %collective-permute-start.1 = (bf16[2,128,256]{2,1,0:T(8,128)(2,1)}, bf16[2,128,256]{2,1,0:T(8,128)(2,1)S(1)}, u32[]{:S(2)}, u32[]{:S(2)}) collective-permute-start(bf16[2,128,256]{2,1,0:T(8,128)(2,1)} %collective-permute-done), channel_id=1, source_target_pairs={{0,4},{4,8},{8,12},{12,16},{16,20},{20,24},{24,28},{28,32},{32,36}... | collective-permute-start | bytes 393224 | tf_op jit(solution)/shard_map/ppermute | solution.py:13
  42.0 11.3 %collective-permute-start.3 = (bf16[2,128,256]{2,1,0:T(8,128)(2,1)}, bf16[2,128,256]{2,1,0:T(8,128)(2,1)S(1)}, u32[]{:S(2)}, u32[]{:S(2)}) collective-permute-start(bf16[2,128,256]{2,1,0:T(8,128)(2,1)} %collective-permute-done.2), channel_id=1, source_target_pairs={{0,508},{4,0},{8,4},{12,8},{16,12},{20,16},{24,20},{28,24},{32,28}... | collective-permute-start | bytes 393224 | tf_op jit(solution)/shard_map/ppermute | solution.py:13
  54.6 0.8 copy-start.11
  55.5 0.9 copy-start.10
  56.6 0.9 copy-start.12
  59.6 0.8 copy-start.9
  60.6 13.6 %collective-permute-start.4 = (bf16[2,128,256]{1,2,0:T(8,128)(2,1)S(1)}, bf16[2,128,256]{1,2,0:T(8,128)(2,1)S(1)}, u32[]{:S(2)}, u32[]{:S(2)}) collective-permute-start(bf16[2,128,256]{1,2,0:T(8,128)(2,1)S(1)} %pad_maximum_fusion.1), channel_id=1, source_target_pairs={{0,4},{4,8},{8,12},{12,16},{16,20},{20,24},{24,28},{28,32},{32,36}... | collective-permute-start | bytes 393224 | tf_op jit(solution)/shard_map/ppermute | solution.py:13
  63.0 9.7 %copy-start.5 = (bf16[128,256]{0,1:T(8,128)(2,1)S(1)}, bf16[128,256]{0,1:T(8,128)(2,1)}, u32[]{:S(2)}) copy-start(bf16[128,256]{0,1:T(8,128)(2,1)} %copy-done.4) | copy-start | bytes 196612
  63.0 13.5 %collective-permute-start.6 = (bf16[2,128,256]{1,2,0:T(8,128)(2,1)S(1)}, bf16[2,128,256]{1,2,0:T(8,128)(2,1)S(1)}, u32[]{:S(2)}, u32[]{:S(2)}) collective-permute-start(bf16[2,128,256]{1,2,0:T(8,128)(2,1)S(1)} %pad_maximum_fusion.2), channel_id=1, source_target_pairs={{0,508},{4,0},{8,4},{12,8},{16,12},{20,16},{24,20},{28,24},{32,28}... | collective-permute-start | bytes 393224 | tf_op jit(solution)/shard_map/ppermute | solution.py:13
  72.9 0.9 copy-start.7
  74.3 7.1 %collective-permute-start.5 = (f32[2,128,256]{1,2,0:T(8,128)S(1)}, f32[2,128,256]{1,2,0:T(8,128)S(1)}, u32[]{:S(2)}, u32[]{:S(2)}) collective-permute-start(f32[2,128,256]{1,2,0:T(8,128)S(1)} %maximum_add_fusion.1), channel_id=1, source_target_pairs={{0,504},{4,508},{8,0},{12,4},{16,8},{20,12},{24,16},{28,20},{32,24... | collective-permute-start | bytes 786440 | tf_op jit(solution)/shard_map/ppermute | solution.py:13
  76.6 10.4 %collective-permute-start.7 = (f32[2,128,256]{1,2,0:T(8,128)S(1)}, f32[2,128,256]{1,2,0:T(8,128)S(1)}, u32[]{:S(2)}, u32[]{:S(2)}) collective-permute-start(f32[2,128,256]{1,2,0:T(8,128)S(1)} %maximum_add_fusion.2), channel_id=1, source_target_pairs={{0,8},{4,12},{8,16},{12,20},{16,24},{20,28},{24,32},{28,36},{32,40... | collective-permute-start | bytes 786440 | tf_op jit(solution)/shard_map/ppermute | solution.py:13
  80.2 6.9 %copy-start.2 = (bf16[1024,256]{1,0:T(8,128)(2,1)S(1)}, bf16[1024,256]{1,0:T(8,128)(2,1)}, u32[]{:S(2)}) copy-start(bf16[1024,256]{1,0:T(8,128)(2,1)} %param.12) | copy-start | bytes 1572868
  (1 other events, 0.7 us)
Sparse Core Ops, SparseCore 0:
  88.6 26.1 reduce-scatter.1
where the time goes:
time: 124 us; the launch traced here: 123 us
  starting transfers between devices  46.4 us (37%)
  waiting for transfers between devices  35 us (28%)
  between operations  14 us (11%)
  local copies, waits for them, and re-layouts  13.5 us (11%)
  matrix products  11.5 us (9%)
  other arithmetic  2.81 us (2%)
    ppermute x8, starting transfers between devices, from_behind(): return lax.ppermute(x, axis, [(i, (i + by) % peers) for i in range(peers)])  46.4 us
    reduce_scatter x1, waiting for transfers between devices, body(): lax.psum_scatter(partial_sum, 'head', scatter_dimension=1, tiled=True)  26.3 us
    ppermute x8, waiting for transfers between devices, from_behind(): return lax.ppermute(x, axis, [(i, (i + by) % peers) for i in range(peers)])  8.69 us
    unnamed x32, local copies, waits for them, and re-layouts  4.49 us
    slice x6, local copies, waits for them, and re-layouts, body(): value3 = window[offset][1].reshape(row_count, head_count, HEAD_DIM)  3.35 us
  transfers between devices with their start and end apart: 9, of which 5 were waited for; matrix products, arithmetic and copies ran while one was open for 9% of the time, Pallas kernels for 0%

commit v1 on v0

v1 whole, which is shorter than its diff:
```python
import functools
import math

import jax
import jax.numpy as jnp
from jax import lax
from jax.experimental import pallas as pl
from jax.experimental.pallas import tpu as pltpu
from jax.sharding import PartitionSpec as P

HEAD_DIM = 64
REACH = 2
GROUP = 32
WIDTH = 2 * REACH + 1
PAIR = 2 * HEAD_DIM
LOG2E = math.log2(math.e)
MESH = pl.DeviceIdType.MESH
F32 = jnp.float32
BF16 = jnp.bfloat16
NEAR = (1, -1, 2, -2)


def dot_nn(a, b):
    return lax.dot_general(a, b, (((1,), (0,)), ((), ())), preferred_element_type=F32)


def dot_nt(a, b):
    return lax.dot_general(a, b, (((1,), (1,)), ((), ())), preferred_element_type=F32)


def kernel(
    nb,
    x_hbm, g_hbm, wq_hbm, wk_hbm, wv_hbm, wo_hbm, bins_hbm, table_hbm, hid_hbm,
    out_ref,
    x, g, wq, wk, wv, wo, bins, table, hid,
    kv, qg, qbd, gbd, ew, dp, s2, dp2, bias, st_src, st_in, dk, dv, part, red_src, red_in,
    in_sem, kv_send, kv_recv, qg_send, qg_recv, st_send, st_recv, red_send, red_recv,
):
    rows = x.shape[0]
    feats = wq.shape[1]
    pairs = feats // PAIR
    groups = rows // GROUP
    me = lax.axis_index("blk")
    head = lax.axis_index("head")
    peers = (lax.rem(head + 2, 4), 3 - head, head + 1 - 2 * lax.rem(head, 2))

    loads = [
        pltpu.make_async_copy(src, dst, in_sem.at[i])
        for i, (src, dst) in enumerate(
            (
                (x_hbm, x), (wk_hbm, wk), (wv_hbm, wv), (wq_hbm, wq), (g_hbm, g), (wo_hbm, wo),
                (bins_hbm, bins), (table_hbm, table), (hid_hbm, hid),
            )
        )
    ]
    for load in loads:
        load.start()

    def block(by):
        return lax.rem(me + (by + nb), nb)

    barrier = pltpu.get_barrier_semaphore()
    for by in NEAR:
        pl.semaphore_signal(barrier, inc=1, device_id=(block(by), head), device_id_type=MESH)
    for peer in peers:
        pl.semaphore_signal(barrier, inc=1, device_id=(me, peer), device_id_type=MESH)

    def to_block(src, dst, send, recv, i):
        by = NEAR[i]
        return pltpu.make_async_remote_copy(
            src_ref=src,
            dst_ref=dst.at[REACH - by],
            send_sem=send.at[i],
            recv_sem=recv.at[REACH - by],
            device_id=(block(by), head),
            device_id_type=MESH,
        )

    def wait_from(copies, slot):
        copies[NEAR.index(REACH - slot)].wait_recv()

    loads[0].wait()
    loads[1].wait()
    kv[REACH, 0] = dot_nn(x[...], wk[...]).astype(BF16)
    loads[2].wait()
    kv[REACH, 1] = dot_nn(x[...], wv[...]).astype(BF16)
    pl.semaphore_wait(barrier, len(NEAR) + len(peers))
    kv_out = [to_block(kv.at[REACH], kv, kv_send, kv_recv, i) for i in range(len(NEAR))]
    for copy in kv_out:
        copy.start()
    loads[3].wait()
    qg[REACH, 0] = (dot_nn(x[...], wq[...]).astype(BF16).astype(F32) * (HEAD_DIM**-0.5)).astype(BF16)
    loads[4].wait()
    loads[5].wait()
    qg[REACH, 1] = dot_nt(g[...], wo[...]).astype(BF16)
    qg_out = [to_block(qg.at[REACH], qg, qg_send, qg_recv, i) for i in range(len(NEAR))]
    for copy in qg_out:
        copy.start()

    low_lane = lax.broadcasted_iota(jnp.int32, (rows, PAIR), 1) < HEAD_DIM
    zero = jnp.zeros((rows, PAIR), BF16)

    def spread(slot):
        for pr in range(pairs):
            cols = pl.ds(pr * PAIR, PAIR)
            for which, dst in ((0, qbd), (1, gbd)):
                both = qg[slot, which, :, cols]
                dst[slot, pr, pl.ds(0, rows), :] = jnp.where(low_lane, both, zero)
                dst[slot, pr, pl.ds(rows, rows), :] = jnp.where(low_lane, zero, both)

    spread(REACH)

    loads[6].wait()
    loads[7].wait()
    loads[8].wait()
    lane_group = lax.broadcasted_iota(jnp.int32, (1, rows), 1) // GROUP

    def bias_rows(slot, carry):
        for h in range(2 * pairs):
            lines = []
            for kg in range(groups):
                line = jnp.zeros((1, rows), F32)
                for gr in range(groups):
                    line = jnp.where(lane_group == gr, table[hid[h], bins[gr, slot * groups + kg]], line)
                lines.append(line)
            bias[slot, h // 2, :, pl.ds((h % 2) * rows, rows)] = jnp.concatenate(lines, axis=0) * LOG2E
        return carry

    lax.fori_loop(0, WIDTH, bias_rows, 0)

    def grouped(tile):
        return tile.reshape(groups, GROUP, 2 * rows)

    stats = {}

    def key_tile(slot):
        for pr in range(pairs):
            cols = pl.ds(pr * PAIR, PAIR)
            score = dot_nt(kv[slot, 0, :, cols], qbd[REACH, pr])
            weigh = dot_nt(kv[slot, 1, :, cols], gbd[REACH, pr])
            shift = bias[slot, pr]
            logit = grouped(score) * LOG2E + shift[:, None, :]
            peak = jnp.max(logit, axis=(0, 1), keepdims=True)
            expo = jnp.exp2(logit - peak).reshape(rows, 2 * rows)
            ew[slot, pr] = expo
            dp[slot, pr] = weigh
            total = jnp.sum(expo, axis=0, keepdims=True)
            cross = jnp.sum(expo * weigh, axis=0, keepdims=True)
            stats[slot, pr] = (peak.reshape(1, 2 * rows), total, cross)

    order = (REACH, 0, 2 * REACH, 1, 3)
    for slot in order:
        if slot != REACH:
            wait_from(kv_out, slot)
        key_tile(slot)

    scale = {}
    dots = []
    for pr in range(pairs):
        top = functools.reduce(jnp.maximum, [stats[s, pr][0] for s in range(WIDTH)])
        lift = [jnp.exp2(stats[s, pr][0] - top) for s in range(WIDTH)]
        total = sum(stats[s, pr][1] * lift[s] for s in range(WIDTH))
        cross = sum(stats[s, pr][2] * lift[s] for s in range(WIDTH))
        inverse = 1.0 / total
        lse = top + jnp.log2(total)
        row_dot = cross * inverse
        dots.append(row_dot)
        for s in range(WIDTH):
            scale[s, pr] = lift[s] * inverse
            if s != REACH:
                st_src[s, pr, pl.ds(0, groups), :] = bias[s, pr] - lse
                st_src[s, pr, pl.ds(groups, groups), :] = jnp.broadcast_to(row_dot, (groups, 2 * rows))
    st_out = [to_block(st_src.at[REACH + NEAR[i]], st_in, st_send, st_recv, i) for i in range(len(NEAR))]
    for copy in st_out:
        copy.start()

    low_row = lax.broadcasted_iota(jnp.int32, (PAIR, rows), 0) < HEAD_DIM
    grad_query = []
    for pr in range(pairs):
        cols = pl.ds(pr * PAIR, PAIR)
        acc = jnp.zeros((PAIR, rows), F32)
        for slot in order:
            prob = ew[slot, pr] * scale[slot, pr]
            grad_score = (prob * (dp[slot, pr] - dots[pr])).astype(BF16)
            key_t = kv[slot, 0, :, cols].astype(F32).T
            key_m = jnp.concatenate(
                [jnp.where(low_row, key_t, 0.0), jnp.where(low_row, 0.0, key_t)], axis=1
            ).astype(BF16)
            stacked = jnp.concatenate([grad_score[:, :rows], grad_score[:, rows:]], axis=0)
            acc = acc + dot_nn(key_m, stacked)
            if slot == REACH:
                dk[pr] = dot_nn(grad_score, qbd[slot, pr])
                dv[pr] = dot_nn(prob.astype(BF16), gbd[slot, pr])
        grad_query.append((acc * (HEAD_DIM**-0.5)).T.astype(BF16))
    query_all = jnp.concatenate(grad_query, axis=1)
    part[...] = dot_nt(query_all, wq[...])

    others = (0, 2 * REACH, 1, 3)
    for slot in others:
        wait_from(qg_out, slot)
        spread(slot)
        for pr in range(pairs):
            cols = pl.ds(pr * PAIR, PAIR)
            s2[slot, pr] = dot_nt(kv[REACH, 0, :, cols], qbd[slot, pr]) * LOG2E
            dp2[slot, pr] = dot_nt(kv[REACH, 1, :, cols], gbd[slot, pr])

    for slot in others:
        wait_from(st_out, slot)
        for pr in range(pairs):
            shift = st_in[slot, pr, pl.ds(0, groups), :]
            row_dot = st_in[slot, pr, pl.ds(groups, 1), :]
            prob = jnp.exp2(grouped(s2[slot, pr]) + shift[:, None, :]).reshape(rows, 2 * rows)
            grad_score = (prob * (dp2[slot, pr] - row_dot)).astype(BF16)
            dk[pr] += dot_nn(grad_score, qbd[slot, pr])
            dv[pr] += dot_nn(prob.astype(BF16), gbd[slot, pr])

    key_all = jnp.concatenate([dk[pr].astype(BF16) for pr in range(pairs)], axis=1)
    value_all = jnp.concatenate([dv[pr].astype(BF16) for pr in range(pairs)], axis=1)

    def share(j):
        lines = pl.ds(pl.multiple_of(j * feats, feats), feats)
        return (
            part[:, lines]
            + dot_nt(key_all, wk[lines, :])
            + dot_nt(value_all, wv[lines, :])
        )

    red_out = []
    for i, peer in enumerate(peers):
        red_src[i] = share(peer).astype(BF16)
        copy = pltpu.make_async_remote_copy(
            src_ref=red_src.at[i],
            dst_ref=red_in.at[i],
            send_sem=red_send.at[i],
            recv_sem=red_recv.at[i],
            device_id=(me, peer),
            device_id_type=MESH,
        )
        copy.start()
        red_out.append(copy)
    total = share(head)
    for i in (2, 0, 1):
        red_out[i].wait_recv()
        total = total + red_in[i].astype(F32)
    out_ref[...] = total.astype(out_ref.dtype)
    for copy in (*kv_out, *qg_out, *st_out, *red_out):
        copy.wait_send()


def solution(mesh):
    nb = mesh.shape["blk"]

    def body(vertices, grad_out, w_query, w_key, w_value, w_out, pair_bins, bias_table, head_index):
        rows, width = vertices.shape
        feats = w_query.shape[1]
        pairs = feats // PAIR
        vmem, smem, dma = pltpu.VMEM, pltpu.SMEM, pltpu.SemaphoreType.DMA
        scratch = [
            vmem((rows, width), BF16),
            vmem((rows, width), BF16),
            vmem((width, feats), BF16),
            vmem((width, feats), BF16),
            vmem((width, feats), BF16),
            vmem((feats, width), BF16),
            smem(pair_bins.shape, jnp.int32),
            smem(bias_table.shape, F32),
            smem(head_index.shape, jnp.int32),
            vmem((WIDTH, 2, rows, feats), BF16),
            vmem((WIDTH, 2, rows, feats), BF16),
            vmem((WIDTH, pairs, 2 * rows, PAIR), BF16),
            vmem((WIDTH, pairs, 2 * rows, PAIR), BF16),
            vmem((WIDTH, pairs, rows, 2 * rows), F32),
            vmem((WIDTH, pairs, rows, 2 * rows), F32),
            vmem((WIDTH, pairs, rows, 2 * rows), F32),
            vmem((WIDTH, pairs, rows, 2 * rows), F32),
            vmem((WIDTH, pairs, rows // GROUP, 2 * rows), F32),
            vmem((WIDTH, pairs, 8, 2 * rows), F32),
            vmem((WIDTH, pairs, 8, 2 * rows), F32),
            vmem((pairs, rows, PAIR), F32),
            vmem((pairs, rows, PAIR), F32),
            vmem((rows, width), F32),
            vmem((3, rows, feats), BF16),
            vmem((3, rows, feats), BF16),
            dma((9,)),
            dma((4,)), dma((WIDTH,)),
            dma((4,)), dma((WIDTH,)),
            dma((4,)), dma((WIDTH,)),
            dma((3,)), dma((3,)),
        ]
        return pl.pallas_call(
            functools.partial(kernel, nb),
            out_shape=jax.ShapeDtypeStruct((rows, feats), BF16),
            in_specs=[pl.BlockSpec(memory_space=pl.ANY)] * 9,
            out_specs=pl.BlockSpec(memory_space=pltpu.VMEM),
            scratch_shapes=scratch,
            compiler_params=pltpu.CompilerParams(
                collective_id=0, has_side_effects=True, vmem_limit_bytes=40 * 2**20
            ),
            name="attend_backward",
        )(vertices, grad_out, w_query, w_key, w_value, w_out, pair_bins, bias_table, head_index)

    in_specs = (
        P("blk", None),
        P("blk", None),
        P(None, "head"),
        P(None, "head"),
        P(None, "head"),
        P("head", None),
        P("blk", None),
        P(),
        P("head"),
    )
    return jax.shard_map(body, mesh=mesh, in_specs=in_specs, out_specs=P("blk", "head"), check_vma=False)
```

time: 124 us -> 45.4 us (0.37)
  starting transfers between devices: 46.4 us -> 0 us
  Pallas kernels: 0 us -> 36.3 us
  waiting for transfers between devices: 35 us -> 0 us
  between operations: 14 us -> 0.02 us
  matrix products: 11.5 us -> 0 us
  local copies, waits for them, and re-layouts: 13.5 us -> 8.71 us
  other arithmetic: 2.81 us -> 0 us
    ppermute x8 -> x0, starting transfers between devices: 46.4 us -> none  [from_behind(): return lax.ppermute(x, axis, [(i, (i + by) % peers) for i in range(peers)])]
    pallas_call x0 -> x1, Pallas kernels: none -> 36.3 us  [body(): pl.pallas_call(functools.partial(kernel, nb), out_shape=jax.ShapeDtypeStr...]
    reduce_scatter x1 -> x0, waiting for transfers between devices: 26.3 us -> none  [body(): lax.psum_scatter(partial_sum, 'head', scatter_dimension=1, tiled=True)]
    dot_general x39 -> x0, matrix products: 11.5 us -> none  [the longest x1 1.45 us: body(): jnp.dot(vertices, w_key, preferred_element_type=jnp.float32)]
    ppermute x8 -> x0, waiting for transfers between devices: 8.69 us -> none  [from_behind(): return lax.ppermute(x, axis, [(i, (i + by) % peers) for i in range(peers)])]
    slice x18 -> x0, local copies, waits for them, and re-layouts: 4.58 us -> none  [the longest x6 3.35 us: body(): value3 = window[offset][1].reshape(row_count, head_count, HEAD_DIM)]
    unnamed x32 -> x19, local copies, waits for them, and re-layouts: 4.49 us -> 8.71 us
    reshape x5 -> x0, local copies, waits for them, and re-layouts: 2.32 us -> none  [spread_bias(): return wide.reshape(count, rows_g * GROUP, cols_g * GROUP)]
  transfers between devices with their start and end apart: 9 -> 0, of which waited for: 5 -> 0; matrix products, arithmetic and copies ran while one was open for 9% -> 0% of each run, Pallas kernels for 0% -> 0%
where the time goes in v1:
time: 45.4 us; the launch traced here: 45 us
  Pallas kernels  36.3 us (80%)
  local copies, waits for them, and re-layouts  8.71 us (19%)
    pallas_call x1, Pallas kernels, body(): pl.pallas_call(functools.partial(kernel, nb), out_shape=jax.ShapeDtypeStr...  36.3 us
    unnamed x19, local copies, waits for them, and re-layouts  8.71 us

profile of v1, /device:TPU:1, one launch (start us, length us, event | category | flops | bytes accessed | tf_op | source)
XLA Modules:
  0.0 45.0 jit_solution(15578006461549558890)
XLA Ops:
  0.0 0.0 copy-start
  0.0 1.0 %copy-done = bf16[1024,256]{1,0:T(8,128)(2,1)S(1)} copy-done((bf16[1024,256]{1,0:T(8,128)(2,1)S(1)}, bf16[1024,256]{1,0:T(8,128)(2,1)}, u32[]{:S(2)}) %copy-start) | copy-done | bytes 524312
  1.0 0.0 copy-start.1
  1.0 1.0 %copy-done.1 = bf16[1024,256]{1,0:T(8,128)(2,1)S(1)} copy-done((bf16[1024,256]{1,0:T(8,128)(2,1)S(1)}, bf16[1024,256]{1,0:T(8,128)(2,1)}, u32[]{:S(2)}) %copy-start.1) | copy-done | bytes 524312
  2.1 0.0 copy-start.2
  2.1 1.0 %copy-done.2 = bf16[1024,256]{1,0:T(8,128)(2,1)S(1)} copy-done((bf16[1024,256]{1,0:T(8,128)(2,1)S(1)}, bf16[1024,256]{1,0:T(8,128)(2,1)}, u32[]{:S(2)}) %copy-start.2) | copy-done | bytes 524312
  3.1 0.0 copy-start.3
  3.1 1.0 %copy-done.3 = bf16[256,1024]{1,0:T(8,128)(2,1)S(1)} copy-done((bf16[256,1024]{1,0:T(8,128)(2,1)S(1)}, bf16[256,1024]{1,0:T(8,128)(2,1)}, u32[]{:S(2)}) %copy-start.3) | copy-done | bytes 524312
  4.2 0.0 copy-start.4
  4.2 0.9 %copy-done.4 = bf16[128,1024]{1,0:T(8,128)(2,1)S(1)} copy-done((bf16[128,1024]{1,0:T(8,128)(2,1)S(1)}, bf16[128,1024]{1,0:T(8,128)(2,1)}, u32[]{:S(2)}) %copy-start.4) | copy-done | bytes 262168
  5.1 0.0 copy-start.5
  5.1 0.9 %copy-done.5 = bf16[128,1024]{1,0:T(8,128)(2,1)S(1)} copy-done((bf16[128,1024]{1,0:T(8,128)(2,1)S(1)}, bf16[128,1024]{1,0:T(8,128)(2,1)}, u32[]{:S(2)}) %copy-start.5) | copy-done | bytes 262168
  6.1 0.0 copy-start.6
  6.1 0.7 %copy-done.6 = s32[4,20]{1,0:T(4,128)S(1)} copy-done((s32[4,20]{1,0:T(4,128)S(1)}, s32[4,20]{1,0:T(4,128)}, u32[]{:S(2)}) %copy-start.6) | copy-done | bytes 344
  6.8 0.0 copy-start.7
  6.8 0.7 %copy-done.7 = f32[4,32]{1,0:T(4,128)S(1)} copy-done((f32[4,32]{1,0:T(4,128)S(1)}, f32[4,32]{1,0:T(4,128)}, u32[]{:S(2)}) %copy-start.7) | copy-done | bytes 536
  7.4 0.0 copy-start.8
  7.4 0.7 %copy-done.8 = s32[4]{0:T(128)S(1)} copy-done((s32[4]{0:T(128)S(1)}, s32[4]{0:T(128)}, u32[]{:S(2)}) %copy-start.8) | copy-done | bytes 40
  8.1 36.3 %attend_backward.1 = bf16[128,256]{1,0:T(8,128)(2,1)S(1)} custom-call(bf16[128,1024]{1,0:T(8,128)(2,1)S(1)} %copy-done.4, bf16[128,1024]{1,0:T(8,128)(2,1)S(1)} %copy-done.5, bf16[1024,256]{1,0:T(8,128)(2,1)S(1)} %copy-done, bf16[1024,256]{1,0:T(8,128)(2,1)S(1)} %copy-done.1, bf16[1024,256]{1,0:T(8,128)(2,1)S(1)} %copy-done.2, ...), custom_call_target="tpu_custom_call" | custom-call | tf_op jit(solution)/shard_map/attend_backward/pallas_call | solution.py:290
  44.4 0.6 %copy.11 = bf16[128,256]{1,0:T(8,128)(2,1)} copy(bf16[128,256]{1,0:T(8,128)(2,1)S(1)} %attend_backward.1) | data formatting | bytes 131072
Async XLA Ops:
  0.0 1.0 %copy-start = (bf16[1024,256]{1,0:T(8,128)(2,1)S(1)}, bf16[1024,256]{1,0:T(8,128)(2,1)}, u32[]{:S(2)}) copy-start(bf16[1024,256]{1,0:T(8,128)(2,1)} %wq_hbm.1) | copy-start | bytes 1572868
  1.0 1.0 %copy-start.1 = (bf16[1024,256]{1,0:T(8,128)(2,1)S(1)}, bf16[1024,256]{1,0:T(8,128)(2,1)}, u32[]{:S(2)}) copy-start(bf16[1024,256]{1,0:T(8,128)(2,1)} %wk_hbm.1) | copy-start | bytes 1572868
  2.1 1.0 %copy-start.2 = (bf16[1024,256]{1,0:T(8,128)(2,1)S(1)}, bf16[1024,256]{1,0:T(8,128)(2,1)}, u32[]{:S(2)}) copy-start(bf16[1024,256]{1,0:T(8,128)(2,1)} %wv_hbm.1) | copy-start | bytes 1572868
  3.1 1.0 %copy-start.3 = (bf16[256,1024]{1,0:T(8,128)(2,1)S(1)}, bf16[256,1024]{1,0:T(8,128)(2,1)}, u32[]{:S(2)}) copy-start(bf16[256,1024]{1,0:T(8,128)(2,1)} %wo_hbm.1) | copy-start | bytes 1572868
  4.2 0.9 %copy-start.4 = (bf16[128,1024]{1,0:T(8,128)(2,1)S(1)}, bf16[128,1024]{1,0:T(8,128)(2,1)}, u32[]{:S(2)}) copy-start(bf16[128,1024]{1,0:T(8,128)(2,1)} %x_hbm.1) | copy-start | bytes 786436
  5.1 0.9 %copy-start.5 = (bf16[128,1024]{1,0:T(8,128)(2,1)S(1)}, bf16[128,1024]{1,0:T(8,128)(2,1)}, u32[]{:S(2)}) copy-start(bf16[128,1024]{1,0:T(8,128)(2,1)} %g_hbm.1) | copy-start | bytes 786436
  6.1 0.7 %copy-start.6 = (s32[4,20]{1,0:T(4,128)S(1)}, s32[4,20]{1,0:T(4,128)}, u32[]{:S(2)}) copy-start(s32[4,20]{1,0:T(4,128)} %bins_hbm.1) | copy-start | bytes 964
  6.8 0.7 %copy-start.7 = (f32[4,32]{1,0:T(4,128)S(1)}, f32[4,32]{1,0:T(4,128)}, u32[]{:S(2)}) copy-start(f32[4,32]{1,0:T(4,128)} %table_hbm.1) | copy-start | bytes 1540
  7.4 0.7 %copy-start.8 = (s32[4]{0:T(128)S(1)}, s32[4]{0:T(128)}, u32[]{:S(2)}) copy-start(s32[4]{0:T(128)} %hid_hbm.1) | copy-start | bytes 52

commit v2 on v1

--- a/solution.py
+++ b/solution.py
@@ -149,10 +149,15 @@
             stats[slot, pr] = (peak.reshape(1, 2 * rows), total, cross)
 
     order = (REACH, 0, 2 * REACH, 1, 3)
-    for slot in order:
-        if slot != REACH:
-            wait_from(kv_out, slot)
-        key_tile(slot)
+    key_tile(REACH)
+    wait_from(kv_out, order[1])
+    key_tile(order[1])
+    wait_from(kv_out, order[2])
+    key_tile(order[2])
+    wait_from(kv_out, order[3])
+    key_tile(order[3])
+    wait_from(kv_out, order[4])
+    key_tile(order[4])
 
     scale = {}
     dots = []
@@ -204,8 +209,7 @@
             s2[slot, pr] = dot_nt(kv[REACH, 0, :, cols], qbd[slot, pr]) * LOG2E
             dp2[slot, pr] = dot_nt(kv[REACH, 1, :, cols], gbd[slot, pr])
 
-    for slot in others:
-        wait_from(st_out, slot)
+    def query_tile(slot):
         for pr in range(pairs):
             shift = st_in[slot, pr, pl.ds(0, groups), :]
             row_dot = st_in[slot, pr, pl.ds(groups, 1), :]
@@ -214,6 +218,14 @@
             dk[pr] += dot_nn(grad_score, qbd[slot, pr])
             dv[pr] += dot_nn(prob.astype(BF16), gbd[slot, pr])
 
+    wait_from(st_out, others[0])
+    query_tile(others[0])
+    wait_from(st_out, others[1])
+    query_tile(others[1])
+    wait_from(st_out, others[2])
+    query_tile(others[2])
+    wait_from(st_out, others[3])
+    query_tile(others[3])
     key_all = jnp.concatenate([dk[pr].astype(BF16) for pr in range(pairs)], axis=1)
     value_all = jnp.concatenate([dv[pr].astype(BF16) for pr in range(pairs)], axis=1)
 
@@ -290,11 +302,11 @@
         return pl.pallas_call(
             functools.partial(kernel, nb),
             out_shape=jax.ShapeDtypeStruct((rows, feats), BF16),
-            in_specs=[pl.BlockSpec(memory_space=pl.ANY)] * 9,
+            in_specs=[pl.BlockSpec(memory_space=pltpu.MemorySpace.HBM)] * 9,
             out_specs=pl.BlockSpec(memory_space=pltpu.VMEM),
             scratch_shapes=scratch,
             compiler_params=pltpu.CompilerParams(
-                collective_id=0, has_side_effects=True, vmem_limit_bytes=40 * 2**20
+                collective_id=0, has_side_effects=True, vmem_limit_bytes=63 * 2**20 + 2**19
             ),
             name="attend_backward",
         )(vertices, grad_out, w_query, w_key, w_value, w_out, pair_bins, bias_table, head_index)

time: 45.4 us -> 38.4 us (0.85)
  local copies, waits for them, and re-layouts: 8.71 us -> 1.47 us
    unnamed x19 -> x1, local copies, waits for them, and re-layouts: 8.71 us -> 1.47 us
where the time goes in v2:
time: 38.4 us; the launch traced here: 38.2 us
  Pallas kernels  36.7 us (96%)
  local copies, waits for them, and re-layouts  1.47 us (4%)
    pallas_call x1, Pallas kernels, body(): pl.pallas_call(functools.partial(kernel, nb), out_shape=jax.ShapeDtypeStr...  36.7 us
    unnamed x1, local copies, waits for them, and re-layouts  1.47 us

profile of v2, /device:TPU:1, one launch (start us, length us, event | category | flops | bytes accessed | tf_op | source)
XLA Modules:
  0.0 38.2 jit_solution(14336429888675096199)
XLA Ops:
  0.0 36.7 %attend_backward.1 = bf16[128,256]{1,0:T(8,128)(2,1)} custom-call(bf16[128,1024]{1,0:T(8,128)(2,1)} %x_hbm.1, bf16[128,1024]{1,0:T(8,128)(2,1)} %g_hbm.1, bf16[1024,256]{1,0:T(8,128)(2,1)} %wq_hbm.1, bf16[1024,256]{1,0:T(8,128)(2,1)} %wk_hbm.1, bf16[1024,256]{1,0:T(8,128)(2,1)} %wv_hbm.1, bf16[256,1024]{1,0:T(8,128)(2,1)} %wo_hbm.1, s32[4,20]{1,0:T(4,128)} %bins_hbm.1, ...), custom_call_target="tpu_custom_call" | custom-call | tf_op jit(solution)/shard_map/attend_backward/pallas_call | solution.py:302
  36.7 1.5 %copy.11 = bf16[128,256]{1,0:T(8,128)(2,1)} copy(bf16[128,256]{1,0:T(8,128)(2,1)} %attend_backward.1) | data formatting | bytes 131072

commit v3 on v2

--- a/solution.py
+++ b/solution.py
@@ -33,8 +33,8 @@
     x_hbm, g_hbm, wq_hbm, wk_hbm, wv_hbm, wo_hbm, bins_hbm, table_hbm, hid_hbm,
     out_ref,
     x, g, wq, wk, wv, wo, bins, table, hid,
-    kv, qg, qbd, gbd, ew, dp, s2, dp2, bias, st_src, st_in, dk, dv, part, red_src, red_in,
-    in_sem, kv_send, kv_recv, qg_send, qg_recv, st_send, st_recv, red_send, red_recv,
+    kv, qg, qbd, gbd, ew, dp, s2, dp2, bias, bias_in, st_src, st_in, dk, dv, part, red_src, red_in,
+    in_sem, kv_send, kv_recv, qg_send, qg_recv, bias_send, bias_recv, st_send, st_recv, red_send, red_recv,
 ):
     rows = x.shape[0]
     feats = wq.shape[1]
@@ -43,6 +43,15 @@
     me = lax.axis_index("blk")
     head = lax.axis_index("head")
     peers = (lax.rem(head + 2, 4), 3 - head, head + 1 - 2 * lax.rem(head, 2))
+
+    def block(by):
+        return lax.rem(me + (by + nb), nb)
+
+    barrier = pltpu.get_barrier_semaphore()
+    for by in NEAR:
+        pl.semaphore_signal(barrier, inc=1, device_id=(block(by), head), device_id_type=MESH)
+    for peer in peers:
+        pl.semaphore_signal(barrier, inc=1, device_id=(me, peer), device_id_type=MESH)
 
     loads = [
         pltpu.make_async_copy(src, dst, in_sem.at[i])
@@ -53,17 +62,8 @@
             )
         )
     ]
-    for load in loads:
+    for load in loads[:3]:
         load.start()
-
-    def block(by):
-        return lax.rem(me + (by + nb), nb)
-
-    barrier = pltpu.get_barrier_semaphore()
-    for by in NEAR:
-        pl.semaphore_signal(barrier, inc=1, device_id=(block(by), head), device_id_type=MESH)
-    for peer in peers:
-        pl.semaphore_signal(barrier, inc=1, device_id=(me, peer), device_id_type=MESH)
 
     def to_block(src, dst, send, recv, i):
         by = NEAR[i]
@@ -81,6 +81,8 @@
 
     loads[0].wait()
     loads[1].wait()
+    for load in loads[3:]:
+        load.start()
     kv[REACH, 0] = dot_nn(x[...], wk[...]).astype(BF16)
     loads[2].wait()
     kv[REACH, 1] = dot_nn(x[...], wv[...]).astype(BF16)
@@ -93,10 +95,6 @@
     loads[4].wait()
     loads[5].wait()
     qg[REACH, 1] = dot_nt(g[...], wo[...]).astype(BF16)
-    qg_out = [to_block(qg.at[REACH], qg, qg_send, qg_recv, i) for i in range(len(NEAR))]
-    for copy in qg_out:
-        copy.start()
-
     low_lane = lax.broadcasted_iota(jnp.int32, (rows, PAIR), 1) < HEAD_DIM
     zero = jnp.zeros((rows, PAIR), BF16)
 
@@ -150,6 +148,12 @@
 
     order = (REACH, 0, 2 * REACH, 1, 3)
     key_tile(REACH)
+    qg_out = [to_block(qg.at[REACH], qg, qg_send, qg_recv, i) for i in range(len(NEAR))]
+    bias_out = [to_block(bias.at[REACH + NEAR[i]], bias_in, bias_send, bias_recv, i) for i in range(len(NEAR))]
+    for copy in kv_out:
+        copy.wait_send()
+    for copy in (*qg_out, *bias_out):
+        copy.start()
     wait_from(kv_out, order[1])
     key_tile(order[1])
     wait_from(kv_out, order[2])
@@ -172,10 +176,11 @@
         dots.append(row_dot)
         for s in range(WIDTH):
             scale[s, pr] = lift[s] * inverse
-            if s != REACH:
-                st_src[s, pr, pl.ds(0, groups), :] = bias[s, pr] - lse
-                st_src[s, pr, pl.ds(groups, groups), :] = jnp.broadcast_to(row_dot, (groups, 2 * rows))
-    st_out = [to_block(st_src.at[REACH + NEAR[i]], st_in, st_send, st_recv, i) for i in range(len(NEAR))]
+        for half in range(2):
+            cols = slice(half * rows, (half + 1) * rows)
+            st_src[pl.ds(2 * pr + half, 1), :] = lse[:, cols]
+            st_src[pl.ds(2 * (pairs + pr) + half, 1), :] = row_dot[:, cols]
+    st_out = [to_block(st_src, st_in, st_send, st_recv, i) for i in range(len(NEAR))]
     for copy in st_out:
         copy.start()
 
@@ -203,17 +208,21 @@
     others = (0, 2 * REACH, 1, 3)
     for slot in others:
         wait_from(qg_out, slot)
+        wait_from(bias_out, slot)
         spread(slot)
         for pr in range(pairs):
             cols = pl.ds(pr * PAIR, PAIR)
-            s2[slot, pr] = dot_nt(kv[REACH, 0, :, cols], qbd[slot, pr]) * LOG2E
+            score = dot_nt(kv[REACH, 0, :, cols], qbd[slot, pr])
+            s2[slot, pr] = (grouped(score) * LOG2E + bias_in[slot, pr][:, None, :]).reshape(rows, 2 * rows)
             dp2[slot, pr] = dot_nt(kv[REACH, 1, :, cols], gbd[slot, pr])
 
     def query_tile(slot):
         for pr in range(pairs):
-            shift = st_in[slot, pr, pl.ds(0, groups), :]
-            row_dot = st_in[slot, pr, pl.ds(groups, 1), :]
-            prob = jnp.exp2(grouped(s2[slot, pr]) + shift[:, None, :]).reshape(rows, 2 * rows)
+            lse, row_dot = (
+                jnp.concatenate([st_in[slot, pl.ds(2 * at + half, 1), :] for half in range(2)], axis=1)
+                for at in (pr, pairs + pr)
+            )
+            prob = jnp.exp2(s2[slot, pr] - lse)
             grad_score = (prob * (dp2[slot, pr] - row_dot)).astype(BF16)
             dk[pr] += dot_nn(grad_score, qbd[slot, pr])
             dv[pr] += dot_nn(prob.astype(BF16), gbd[slot, pr])
@@ -255,7 +264,7 @@
         red_out[i].wait_recv()
         total = total + red_in[i].astype(F32)
     out_ref[...] = total.astype(out_ref.dtype)
-    for copy in (*kv_out, *qg_out, *st_out, *red_out):
+    for copy in (*qg_out, *bias_out, *st_out, *red_out):
         copy.wait_send()
 
 
@@ -286,8 +295,9 @@
             vmem((WIDTH, pairs, rows, 2 * rows), F32),
             vmem((WIDTH, pairs, rows, 2 * rows), F32),
             vmem((WIDTH, pairs, rows // GROUP, 2 * rows), F32),
-            vmem((WIDTH, pairs, 8, 2 * rows), F32),
-            vmem((WIDTH, pairs, 8, 2 * rows), F32),
+            vmem((WIDTH, pairs, rows // GROUP, 2 * rows), F32),
+            vmem((4 * pairs, rows), F32),
+            vmem((WIDTH, 4 * pairs, rows), F32),
             vmem((pairs, rows, PAIR), F32),
             vmem((pairs, rows, PAIR), F32),
             vmem((rows, width), F32),
@@ -297,19 +307,22 @@
             dma((4,)), dma((WIDTH,)),
             dma((4,)), dma((WIDTH,)),
             dma((4,)), dma((WIDTH,)),
+            dma((4,)), dma((WIDTH,)),
             dma((3,)), dma((3,)),
         ]
         return pl.pallas_call(
             functools.partial(kernel, nb),
-            out_shape=jax.ShapeDtypeStruct((rows, feats), BF16),
-            in_specs=[pl.BlockSpec(memory_space=pltpu.MemorySpace.HBM)] * 9,
+            out_shape=pltpu.VMEM((rows, feats), BF16),
+            in_specs=[pl.BlockSpec(memory_space=pl.ANY)] * 9,
             out_specs=pl.BlockSpec(memory_space=pltpu.VMEM),
             scratch_shapes=scratch,
             compiler_params=pltpu.CompilerParams(
-                collective_id=0, has_side_effects=True, vmem_limit_bytes=63 * 2**20 + 2**19
+                collective_id=0, has_side_effects=True, vmem_limit_bytes=32 * 2**20
             ),
             name="attend_backward",
-        )(vertices, grad_out, w_query, w_key, w_value, w_out, pair_bins, bias_table, head_index)
+        )(*(pltpu.with_memory_space_constraint(a, pltpu.HBM) for a in (
+            vertices, grad_out, w_query, w_key, w_value, w_out, pair_bins, bias_table, head_index
+        )))
 
     in_specs = (
         P("blk", None),

time: 38.4 us -> 36.5 us (0.951)
  Pallas kernels: 36.7 us -> 35.8 us
  local copies, waits for them, and re-layouts: 1.47 us -> 0.63 us
    pallas_call x1, Pallas kernels: 36.7 us -> 35.8 us  [body(): pl.pallas_call(functools.partial(kernel, nb), out_shape=pltpu.VMEM((rows,...]
    unnamed x1, local copies, waits for them, and re-layouts: 1.47 us -> 0.63 us
where the time goes in v3:
time: 36.5 us; the launch traced here: 36.4 us
  Pallas kernels  35.8 us (98%)
  local copies, waits for them, and re-layouts  0.63 us (2%)
    pallas_call x1, Pallas kernels, body(): pl.pallas_call(functools.partial(kernel, nb), out_shape=pltpu.VMEM((rows,...  35.8 us

profile of v3, /device:TPU:1, one launch (start us, length us, event | category | flops | bytes accessed | tf_op | source)
XLA Modules:
  0.0 36.4 jit_solution(11301389229102160728)
XLA Ops:
  0.0 35.8 %attend_backward.1 = bf16[128,256]{1,0:T(8,128)(2,1)S(1)} custom-call(bf16[128,1024]{1,0:T(8,128)(2,1)} %x_hbm.1, bf16[128,1024]{1,0:T(8,128)(2,1)} %g_hbm.1, bf16[1024,256]{1,0:T(8,128)(2,1)} %wq_hbm.1, bf16[1024,256]{1,0:T(8,128)(2,1)} %wk_hbm.1, bf16[1024,256]{1,0:T(8,128)(2,1)} %wv_hbm.1, bf16[256,1024]{1,0:T(8,128)(2,1)} %wo_hbm.1, s32[4,20]{1,0:T(4,128)} %bins_hbm.1, ...), custom_call_target="tpu_custom_call" | custom-call | tf_op jit(solution)/shard_map/attend_backward/pallas_call | solution.py:313
  35.8 0.6 %copy.11 = bf16[128,256]{1,0:T(8,128)(2,1)} copy(bf16[128,256]{1,0:T(8,128)(2,1)S(1)} %attend_backward.1) | data formatting | bytes 131072

commit v4 on v3

--- a/solution.py
+++ b/solution.py
@@ -17,7 +17,6 @@
 MESH = pl.DeviceIdType.MESH
 F32 = jnp.float32
 BF16 = jnp.bfloat16
-NEAR = (1, -1, 2, -2)
 
 
 def dot_nn(a, b):
@@ -47,8 +46,10 @@
     def block(by):
         return lax.rem(me + (by + nb), nb)
 
+    far = 2 * lax.rem(me, 2) - 1
+    near = (far, -far, REACH, -REACH)
     barrier = pltpu.get_barrier_semaphore()
-    for by in NEAR:
+    for by in near:
         pl.semaphore_signal(barrier, inc=1, device_id=(block(by), head), device_id_type=MESH)
     for peer in peers:
         pl.semaphore_signal(barrier, inc=1, device_id=(me, peer), device_id_type=MESH)
@@ -66,7 +67,7 @@
         load.start()
 
     def to_block(src, dst, send, recv, i):
-        by = NEAR[i]
+        by = near[i]
         return pltpu.make_async_remote_copy(
             src_ref=src,
             dst_ref=dst.at[REACH - by],
@@ -76,8 +77,10 @@
             device_id_type=MESH,
         )
 
-    def wait_from(copies, slot):
-        copies[NEAR.index(REACH - slot)].wait_recv()
+    slots = (REACH, *(REACH - by for by in near))
+
+    def wait_from(copies, tile):
+        copies[tile - 1].wait_recv()
 
     loads[0].wait()
     loads[1].wait()
@@ -86,8 +89,8 @@
     kv[REACH, 0] = dot_nn(x[...], wk[...]).astype(BF16)
     loads[2].wait()
     kv[REACH, 1] = dot_nn(x[...], wv[...]).astype(BF16)
-    pl.semaphore_wait(barrier, len(NEAR) + len(peers))
-    kv_out = [to_block(kv.at[REACH], kv, kv_send, kv_recv, i) for i in range(len(NEAR))]
+    pl.semaphore_wait(barrier, len(near) + len(peers))
+    kv_out = [to_block(kv.at[REACH], kv, kv_send, kv_recv, i) for i in range(len(near))]
     for copy in kv_out:
         copy.start()
     loads[3].wait()
@@ -98,15 +101,15 @@
     low_lane = lax.broadcasted_iota(jnp.int32, (rows, PAIR), 1) < HEAD_DIM
     zero = jnp.zeros((rows, PAIR), BF16)
 
-    def spread(slot):
+    def spread(tile):
         for pr in range(pairs):
             cols = pl.ds(pr * PAIR, PAIR)
             for which, dst in ((0, qbd), (1, gbd)):
-                both = qg[slot, which, :, cols]
-                dst[slot, pr, pl.ds(0, rows), :] = jnp.where(low_lane, both, zero)
-                dst[slot, pr, pl.ds(rows, rows), :] = jnp.where(low_lane, zero, both)
-
-    spread(REACH)
+                both = qg[slots[tile], which, :, cols]
+                dst[tile, pr, pl.ds(0, rows), :] = jnp.where(low_lane, both, zero)
+                dst[tile, pr, pl.ds(rows, rows), :] = jnp.where(low_lane, zero, both)
+
+    spread(0)
 
     loads[6].wait()
     loads[7].wait()
@@ -131,25 +134,26 @@
 
     stats = {}
 
-    def key_tile(slot):
+    def key_tile(tile):
+        slot = slots[tile]
         for pr in range(pairs):
             cols = pl.ds(pr * PAIR, PAIR)
-            score = dot_nt(kv[slot, 0, :, cols], qbd[REACH, pr])
-            weigh = dot_nt(kv[slot, 1, :, cols], gbd[REACH, pr])
+            score = dot_nt(kv[slot, 0, :, cols], qbd[0, pr])
+            weigh = dot_nt(kv[slot, 1, :, cols], gbd[0, pr])
             shift = bias[slot, pr]
             logit = grouped(score) * LOG2E + shift[:, None, :]
             peak = jnp.max(logit, axis=(0, 1), keepdims=True)
             expo = jnp.exp2(logit - peak).reshape(rows, 2 * rows)
-            ew[slot, pr] = expo
-            dp[slot, pr] = weigh
+            ew[tile, pr] = expo
+            dp[tile, pr] = weigh
             total = jnp.sum(expo, axis=0, keepdims=True)
             cross = jnp.sum(expo * weigh, axis=0, keepdims=True)
-            stats[slot, pr] = (peak.reshape(1, 2 * rows), total, cross)
-
-    order = (REACH, 0, 2 * REACH, 1, 3)
-    key_tile(REACH)
-    qg_out = [to_block(qg.at[REACH], qg, qg_send, qg_recv, i) for i in range(len(NEAR))]
-    bias_out = [to_block(bias.at[REACH + NEAR[i]], bias_in, bias_send, bias_recv, i) for i in range(len(NEAR))]
+            stats[tile, pr] = (peak.reshape(1, 2 * rows), total, cross)
+
+    order = (0, 3, 4, 1, 2)
+    key_tile(0)
+    qg_out = [to_block(qg.at[REACH], qg, qg_send, qg_recv, i) for i in range(len(near))]
+    bias_out = [to_block(bias.at[REACH + near[i]], bias_in, bias_send, bias_recv, i) for i in range(len(near))]
     for copy in kv_out:
         copy.wait_send()
     for copy in (*qg_out, *bias_out):
@@ -180,7 +184,7 @@
             cols = slice(half * rows, (half + 1) * rows)
             st_src[pl.ds(2 * pr + half, 1), :] = lse[:, cols]
             st_src[pl.ds(2 * (pairs + pr) + half, 1), :] = row_dot[:, cols]
-    st_out = [to_block(st_src, st_in, st_send, st_recv, i) for i in range(len(NEAR))]
+    st_out = [to_block(st_src, st_in, st_send, st_recv, i) for i in range(len(near))]
     for copy in st_out:
         copy.start()
 
@@ -189,43 +193,45 @@
     for pr in range(pairs):
         cols = pl.ds(pr * PAIR, PAIR)
         acc = jnp.zeros((PAIR, rows), F32)
-        for slot in order:
-            prob = ew[slot, pr] * scale[slot, pr]
-            grad_score = (prob * (dp[slot, pr] - dots[pr])).astype(BF16)
-            key_t = kv[slot, 0, :, cols].astype(F32).T
+        for tile in order:
+            prob = ew[tile, pr] * scale[tile, pr]
+            grad_score = (prob * (dp[tile, pr] - dots[pr])).astype(BF16)
+            key_t = kv[slots[tile], 0, :, cols].astype(F32).T
             key_m = jnp.concatenate(
                 [jnp.where(low_row, key_t, 0.0), jnp.where(low_row, 0.0, key_t)], axis=1
             ).astype(BF16)
             stacked = jnp.concatenate([grad_score[:, :rows], grad_score[:, rows:]], axis=0)
             acc = acc + dot_nn(key_m, stacked)
-            if slot == REACH:
-                dk[pr] = dot_nn(grad_score, qbd[slot, pr])
-                dv[pr] = dot_nn(prob.astype(BF16), gbd[slot, pr])
+            if tile == 0:
+                dk[pr] = dot_nn(grad_score, qbd[0, pr])
+                dv[pr] = dot_nn(prob.astype(BF16), gbd[0, pr])
         grad_query.append((acc * (HEAD_DIM**-0.5)).T.astype(BF16))
     query_all = jnp.concatenate(grad_query, axis=1)
     part[...] = dot_nt(query_all, wq[...])
 
-    others = (0, 2 * REACH, 1, 3)
-    for slot in others:
-        wait_from(qg_out, slot)
-        wait_from(bias_out, slot)
-        spread(slot)
+    others = (3, 4, 1, 2)
+    for tile in others:
+        slot = slots[tile]
+        wait_from(qg_out, tile)
+        wait_from(bias_out, tile)
+        spread(tile)
         for pr in range(pairs):
             cols = pl.ds(pr * PAIR, PAIR)
-            score = dot_nt(kv[REACH, 0, :, cols], qbd[slot, pr])
-            s2[slot, pr] = (grouped(score) * LOG2E + bias_in[slot, pr][:, None, :]).reshape(rows, 2 * rows)
-            dp2[slot, pr] = dot_nt(kv[REACH, 1, :, cols], gbd[slot, pr])
-
-    def query_tile(slot):
+            score = dot_nt(kv[REACH, 0, :, cols], qbd[tile, pr])
+            s2[tile, pr] = (grouped(score) * LOG2E + bias_in[slot, pr][:, None, :]).reshape(rows, 2 * rows)
+            dp2[tile, pr] = dot_nt(kv[REACH, 1, :, cols], gbd[tile, pr])
+
+    def query_tile(tile):
+        slot = slots[tile]
         for pr in range(pairs):
             lse, row_dot = (
                 jnp.concatenate([st_in[slot, pl.ds(2 * at + half, 1), :] for half in range(2)], axis=1)
                 for at in (pr, pairs + pr)
             )
-            prob = jnp.exp2(s2[slot, pr] - lse)
-            grad_score = (prob * (dp2[slot, pr] - row_dot)).astype(BF16)
-            dk[pr] += dot_nn(grad_score, qbd[slot, pr])
-            dv[pr] += dot_nn(prob.astype(BF16), gbd[slot, pr])
+            prob = jnp.exp2(s2[tile, pr] - lse)
+            grad_score = (prob * (dp2[tile, pr] - row_dot)).astype(BF16)
+            dk[pr] += dot_nn(grad_score, qbd[tile, pr])
+            dv[pr] += dot_nn(prob.astype(BF16), gbd[tile, pr])
 
     wait_from(st_out, others[0])
     query_tile(others[0])

time: 36.5 us -> 36.3 us (level)
  no operation moved by 1% of the time
where the time goes in v4:
time: 36.3 us; the launch traced here: 36.2 us
  Pallas kernels  35.5 us (98%)
  local copies, waits for them, and re-layouts  0.63 us (2%)
    pallas_call x1, Pallas kernels, body(): pl.pallas_call(functools.partial(kernel, nb), out_shape=pltpu.VMEM((rows,...  35.5 us

profile of v4, /device:TPU:1, one launch (start us, length us, event | category | flops | bytes accessed | tf_op | source)
XLA Modules:
  0.0 36.2 jit_solution(8447731393986907945)
XLA Ops:
  0.0 35.5 %attend_backward.1 = bf16[128,256]{1,0:T(8,128)(2,1)S(1)} custom-call(bf16[128,1024]{1,0:T(8,128)(2,1)} %x_hbm.1, bf16[128,1024]{1,0:T(8,128)(2,1)} %g_hbm.1, bf16[1024,256]{1,0:T(8,128)(2,1)} %wq_hbm.1, bf16[1024,256]{1,0:T(8,128)(2,1)} %wk_hbm.1, bf16[1024,256]{1,0:T(8,128)(2,1)} %wv_hbm.1, bf16[256,1024]{1,0:T(8,128)(2,1)} %wo_hbm.1, s32[4,20]{1,0:T(4,128)} %bins_hbm.1, ...), custom_call_target="tpu_custom_call" | custom-call | tf_op jit(solution)/shard_map/attend_backward/pallas_call | solution.py:319
  35.5 0.6 %copy.11 = bf16[128,256]{1,0:T(8,128)(2,1)} copy(bf16[128,256]{1,0:T(8,128)(2,1)S(1)} %attend_backward.1) | data formatting | bytes 131072

commit v5 on v4

--- a/solution.py
+++ b/solution.py
@@ -32,7 +32,7 @@
     x_hbm, g_hbm, wq_hbm, wk_hbm, wv_hbm, wo_hbm, bins_hbm, table_hbm, hid_hbm,
     out_ref,
     x, g, wq, wk, wv, wo, bins, table, hid,
-    kv, qg, qbd, gbd, ew, dp, s2, dp2, bias, bias_in, st_src, st_in, dk, dv, part, red_src, red_in,
+    kv, qg, qbd, gbd, ew, dp, s2, dp2, bias, bias_in, st_src, st_in, dk, dv, part, red_src, red_in, turned,
     in_sem, kv_send, kv_recv, qg_send, qg_recv, bias_send, bias_recv, st_send, st_recv, red_send, red_recv,
 ):
     rows = x.shape[0]
@@ -162,6 +162,10 @@
     key_tile(order[1])
     wait_from(kv_out, order[2])
     key_tile(order[2])
+    for j in range(x.shape[1] // feats):
+        lines = pl.ds(j * feats, feats)
+        turned[j, pl.ds(0, feats), :] = wk[lines, :].T
+        turned[j, pl.ds(feats, feats), :] = wv[lines, :].T
     wait_from(kv_out, order[3])
     key_tile(order[3])
     wait_from(kv_out, order[4])
@@ -244,13 +248,11 @@
     key_all = jnp.concatenate([dk[pr].astype(BF16) for pr in range(pairs)], axis=1)
     value_all = jnp.concatenate([dv[pr].astype(BF16) for pr in range(pairs)], axis=1)
 
+    both_all = jnp.concatenate([key_all, value_all], axis=1)
+
     def share(j):
         lines = pl.ds(pl.multiple_of(j * feats, feats), feats)
-        return (
-            part[:, lines]
-            + dot_nt(key_all, wk[lines, :])
-            + dot_nt(value_all, wv[lines, :])
-        )
+        return part[:, lines] + dot_nn(both_all, turned[j])
 
     red_out = []
     for i, peer in enumerate(peers):
@@ -309,6 +311,7 @@
             vmem((rows, width), F32),
             vmem((3, rows, feats), BF16),
             vmem((3, rows, feats), BF16),
+            vmem((width // feats, 2 * feats, feats), BF16),
             dma((9,)),
             dma((4,)), dma((WIDTH,)),
             dma((4,)), dma((WIDTH,)),

time: 36.3 us -> 36.3 us (level)
  no operation moved by 1% of the time
where the time goes in v5:
time: 36.3 us; the launch traced here: 36.1 us
  Pallas kernels  35.5 us (98%)
  local copies, waits for them, and re-layouts  0.63 us (2%)
    pallas_call x1, Pallas kernels, body(): pl.pallas_call(functools.partial(kernel, nb), out_shape=pltpu.VMEM((rows,...  35.5 us

profile of v5, /device:TPU:1, one launch (start us, length us, event | category | flops | bytes accessed | tf_op | source)
XLA Modules:
  0.0 36.1 jit_solution(6478739706086528219)
XLA Ops:
  0.0 35.5 %attend_backward.1 = bf16[128,256]{1,0:T(8,128)(2,1)S(1)} custom-call(bf16[128,1024]{1,0:T(8,128)(2,1)} %x_hbm.1, bf16[128,1024]{1,0:T(8,128)(2,1)} %g_hbm.1, bf16[1024,256]{1,0:T(8,128)(2,1)} %wq_hbm.1, bf16[1024,256]{1,0:T(8,128)(2,1)} %wk_hbm.1, bf16[1024,256]{1,0:T(8,128)(2,1)} %wv_hbm.1, bf16[256,1024]{1,0:T(8,128)(2,1)} %wo_hbm.1, s32[4,20]{1,0:T(4,128)} %bins_hbm.1, ...), custom_call_target="tpu_custom_call" | custom-call | tf_op jit(solution)/shard_map/attend_backward/pallas_call | solution.py:322
  35.5 0.6 %copy.11 = bf16[128,256]{1,0:T(8,128)(2,1)} copy(bf16[128,256]{1,0:T(8,128)(2,1)S(1)} %attend_backward.1) | data formatting | bytes 131072

commit v6 on v5

--- a/solution.py
+++ b/solution.py
@@ -168,22 +168,31 @@
         turned[j, pl.ds(feats, feats), :] = wv[lines, :].T
     wait_from(kv_out, order[3])
     key_tile(order[3])
+    early = []
+    for pr in range(pairs):
+        four = [stats[s, pr] for s in (0, 1, 3, 4)]
+        top = functools.reduce(jnp.maximum, [f[0] for f in four])
+        lift = [jnp.exp2(f[0] - top) for f in four]
+        early.append(
+            (top, sum(f[1] * up for f, up in zip(four, lift)), sum(f[2] * up for f, up in zip(four, lift)))
+        )
     wait_from(kv_out, order[4])
     key_tile(order[4])
 
     scale = {}
     dots = []
     for pr in range(pairs):
-        top = functools.reduce(jnp.maximum, [stats[s, pr][0] for s in range(WIDTH)])
-        lift = [jnp.exp2(stats[s, pr][0] - top) for s in range(WIDTH)]
-        total = sum(stats[s, pr][1] * lift[s] for s in range(WIDTH))
-        cross = sum(stats[s, pr][2] * lift[s] for s in range(WIDTH))
+        last = stats[2, pr]
+        top = jnp.maximum(early[pr][0], last[0])
+        up, down = jnp.exp2(early[pr][0] - top), jnp.exp2(last[0] - top)
+        total = early[pr][1] * up + last[1] * down
+        cross = early[pr][2] * up + last[2] * down
         inverse = 1.0 / total
         lse = top + jnp.log2(total)
         row_dot = cross * inverse
         dots.append(row_dot)
         for s in range(WIDTH):
-            scale[s, pr] = lift[s] * inverse
+            scale[s, pr] = jnp.exp2(stats[s, pr][0] - lse)
         for half in range(2):
             cols = slice(half * rows, (half + 1) * rows)
             st_src[pl.ds(2 * pr + half, 1), :] = lse[:, cols]

time: 36.3 us -> 36.3 us (level)
  no operation moved by 1% of the time
where the time goes in v6:
time: 36.3 us; the launch traced here: 36.1 us
  Pallas kernels  35.5 us (98%)
  local copies, waits for them, and re-layouts  0.63 us (2%)
    pallas_call x1, Pallas kernels, body(): pl.pallas_call(functools.partial(kernel, nb), out_shape=pltpu.VMEM((rows,...  35.5 us

profile of v6, /device:TPU:1, one launch (start us, length us, event | category | flops | bytes accessed | tf_op | source)
XLA Modules:
  0.0 36.1 jit_solution(710442035705620227)
XLA Ops:
  0.0 35.5 %attend_backward.1 = bf16[128,256]{1,0:T(8,128)(2,1)S(1)} custom-call(bf16[128,1024]{1,0:T(8,128)(2,1)} %x_hbm.1, bf16[128,1024]{1,0:T(8,128)(2,1)} %g_hbm.1, bf16[1024,256]{1,0:T(8,128)(2,1)} %wq_hbm.1, bf16[1024,256]{1,0:T(8,128)(2,1)} %wk_hbm.1, bf16[1024,256]{1,0:T(8,128)(2,1)} %wv_hbm.1, bf16[256,1024]{1,0:T(8,128)(2,1)} %wo_hbm.1, s32[4,20]{1,0:T(4,128)} %bins_hbm.1, ...), custom_call_target="tpu_custom_call" | custom-call | tf_op jit(solution)/shard_map/attend_backward/pallas_call | solution.py:331
  35.5 0.6 %copy.11 = bf16[128,256]{1,0:T(8,128)(2,1)} copy(bf16[128,256]{1,0:T(8,128)(2,1)S(1)} %attend_backward.1) | data formatting | bytes 131072
